TPU v7x, 32 devices: a whole 2x2x4 slice. The times are simulated.
32 devices in a mesh: parts: 2 (over x), dom: 8 (over z, y), grp: 2 (over core).
Axes of the slice: x: 2, y: 2, z: 4, core: 2. Of those that a mesh axis runs over, the one named last changes fastest.
Arguments:
- basis: bfloat16 [49152, 768], P(('parts', 'dom', 'grp')), parts along dimension 0, may hold values from -6 to 6
- blocks: bfloat16 [9, 16, 49152], P(None, None, ('parts', 'dom', 'grp')), parts along dimension 2, may hold values from -0.0034179688 to 0.0034179688
- columns: int32 [16, 49152], P(None, ('parts', 'dom', 'grp')), parts along dimension 1, may hold values from 0 to 2015, as said below
- send_list: int32 [32, 6, 80], P(('parts', 'dom', 'grp')), parts along dimension 0, may hold values from 0 to 1535
- send_counts: int32 [32, 6], P(('parts', 'dom', 'grp')), parts along dimension 0, may hold values from 20 to 80, as said below
Outputs:
- reduced_stiffness: float32 [512, 256], P(('parts', 'dom')), parts along dimension 0
There are 2 independent parts, one for each index of `parts`. A program takes and returns all parts, laid end to end along the dimension named above; each array names one. Nothing has to cross between parts.
Inputs may be any that keep to these rules, and one draw needn't show every extreme that they name: `send_counts`: in every draw, within each node group, one partition receives 80 live slots from each of its 6 neighbours. `columns`: block slots of a partition's first 1152 nodes name owned nodes only; the others name owned nodes or live ghost slots.
All inputs are finite; a program needn't handle non-finite values.
Results may differ from a plain program's by a relative error of at most 0.0029.
Values may be sent and summed in bfloat16 or wider, within the bound.
A program may use at most 128 MiB of HBM per device.

v0:
```python
import jax
import jax.numpy as jnp
from jax import lax
from jax.sharding import PartitionSpec as P


def apply_blocks(extended, blocks, columns):
    node_count = columns.shape[1]
    width = extended.shape[1] // 3

    def one_slot(slot_index, accum):
        picked = extended[columns[slot_index]].reshape(node_count, 3, width)
        matrix = blocks[:, slot_index].reshape(3, 3, node_count)
        return accum + jnp.einsum(
            "abn,nbr->nar", matrix, picked, preferred_element_type=jnp.float32
        )

    return lax.fori_loop(
        0, columns.shape[0], one_slot, jnp.zeros((node_count, 3, width), jnp.float32)
    )


def on_device(basis, blocks, columns, send_list, send_counts):
    node_count = basis.shape[0]
    width = basis.shape[1] // 3
    slot_total = send_list.shape[2]
    neighbours = send_list.shape[1]
    reach_count = neighbours // 2
    group_size = lax.axis_size("dom")
    half_way = group_size // 2
    offset_list = [step + 1 for step in range(reach_count - 1)] + [half_way]
    offset_list = offset_list + [-(step + 1) for step in range(reach_count - 1)] + [half_way + 1]
    outgoing = basis[send_list[0]]
    slot_live = jnp.arange(slot_total, dtype=jnp.int32)[None, :] < send_counts[0][:, None]
    outgoing = outgoing * slot_live[:, :, None].astype(jnp.bfloat16)
    position = lax.axis_index("dom")
    offsets = jnp.array(offset_list, dtype=jnp.int32)
    targets = (position + offsets) % group_size
    padded = jnp.zeros((group_size, slot_total, 3 * width), jnp.bfloat16).at[targets].set(outgoing)
    received = lax.all_to_all(padded, "dom", split_axis=0, concat_axis=0, tiled=True)
    ghost_table = received[(position - offsets) % group_size].reshape(-1, 3 * width)
    extended = jnp.concatenate([basis, ghost_table], axis=0)
    kv_float = apply_blocks(extended, blocks, columns)
    kv_rows = kv_float.astype(jnp.bfloat16).reshape(node_count * 3, width)
    left = basis.reshape(node_count * 3, width)
    share = width // group_size
    partial_term = lax.dot_general(
        left, kv_rows, (((0,), (0,)), ((), ())), preferred_element_type=jnp.float32
    )
    summed = lax.psum(partial_term, ("dom", "grp"))
    return lax.dynamic_slice_in_dim(summed, lax.axis_index("dom") * share, share, 0)


def solution(mesh):
    in_specs = (
        P(("parts", "dom", "grp"), None),
        P(None, None, ("parts", "dom", "grp")),
        P(None, ("parts", "dom", "grp")),
        P(("parts", "dom", "grp"), None, None),
        P(("parts", "dom", "grp"), None),
    )
    out_specs = P(("parts", "dom"), None)
    return jax.shard_map(
        on_device, mesh=mesh, in_specs=in_specs, out_specs=out_specs, check_vma=False
    )
```

profile of v0, /device:TPU:0, one launch (start us, length us, event | category | flops | bytes accessed | tf_op | source)
XLA Modules:
  0.0 623.2 jit_solution(18170937315832416597)
XLA Ops:
  19.0 7.3 %all-to-all-start = ((bf16[8,80,768]{2,1,0:T(8,128)(2,1)}), bf16[8,80,768]{2,1,0:T(8,128)(2,1)S(1)}, u32[]{:S(2)}, u32[]{:S(2)}) async-start(bf16[8,80,768]{2,1,0:T(8,128)(2,1)} %scatter_fusion), calls=%async_computation | async-start | bytes 1966080 | tf_op jit(solution)/shard_map/all_to_all | solution.py:40
  30.9 19.7 %all-to-all-done = bf16[8,80,768]{2,1,0:T(8,128)(2,1)S(1)} async-done(((bf16[8,80,768]{2,1,0:T(8,128)(2,1)}), bf16[8,80,768]{2,1,0:T(8,128)(2,1)S(1)}, u32[]{:S(2)}, u32[]{:S(2)}) %all-to-all-start) | async-done | bytes 983072 | tf_op jit(solution)/shard_map/all_to_all | solution.py:40
  54.2 460.5 %while.14 = (s32[]{:T(128)}, f32[1536,3,256]{2,1,0:T(4,128)}, bf16[9,16,1536]{2,0,1:T(8,128)(2,1)}, s32[16,1536]{1,0:T(8,128)}, bf16[2016,768]{1,0:T(8,128)(2,1)S(1)}, /*index=5*/s32[]{:T(128)}, s32[]{:T(128)}) while((s32[]{:T(128)}, f32[1536,3,256]{2,1,0:T(4,128)}, bf16[9,16,1536]{2,0,1:T(8,128)(2,1)}, s32[16,1536]{1,0:T(8,128)}, ...), condition=%wide.region_2.3_spmd.clone, body=%wide.region_1.2_spmd.clone.sunk | while | flops 9443843 | bytes 26178656 | solution.py:18
  73.8 7.4 %select_add_fusion.2 = f32[1536,3,256]{2,1,0:T(4,128)} fusion(f32[1536,3,256]{2,1,0:T(4,128)} %get-tuple-element.177, pred[]{:T(512)S(6)} %compare.5, bf16[3,3,1536]{1,0,2:T(4,128)(2,1)} %copy.17, bf16[1536,3,256]{2,1,0:T(4,128)(2,1)} %copy.19), kind=kOutput, calls=%fused_computation.4.clone.1 | convolution fusion | flops 9437184 | bytes 11824129 | tf_op jit(solution)/shard_map/while/body/eval_jaxpr/abn,nbr->nar/dot_general | solution.py:14
  100.9 9.3 %select_add_fusion.2 = f32[1536,3,256]{2,1,0:T(4,128)} fusion(f32[1536,3,256]{2,1,0:T(4,128)} %get-tuple-element.177, pred[]{:T(512)S(6)} %compare.5, bf16[3,3,1536]{1,0,2:T(4,128)(2,1)} %copy.17, bf16[1536,3,256]{2,1,0:T(4,128)(2,1)} %copy.19), kind=kOutput, calls=%fused_computation.4.clone.1 | convolution fusion | flops 9437184 | bytes 11824129 | tf_op jit(solution)/shard_map/while/body/eval_jaxpr/abn,nbr->nar/dot_general | solution.py:14
  121.0 5.7 copy.19
  129.8 9.3 %select_add_fusion.2 = f32[1536,3,256]{2,1,0:T(4,128)} fusion(f32[1536,3,256]{2,1,0:T(4,128)} %get-tuple-element.177, pred[]{:T(512)S(6)} %compare.5, bf16[3,3,1536]{1,0,2:T(4,128)(2,1)} %copy.17, bf16[1536,3,256]{2,1,0:T(4,128)(2,1)} %copy.19), kind=kOutput, calls=%fused_computation.4.clone.1 | convolution fusion | flops 9437184 | bytes 11824129 | tf_op jit(solution)/shard_map/while/body/eval_jaxpr/abn,nbr->nar/dot_general | solution.py:14
  158.7 9.3 %select_add_fusion.2 = f32[1536,3,256]{2,1,0:T(4,128)} fusion(f32[1536,3,256]{2,1,0:T(4,128)} %get-tuple-element.177, pred[]{:T(512)S(6)} %compare.5, bf16[3,3,1536]{1,0,2:T(4,128)(2,1)} %copy.17, bf16[1536,3,256]{2,1,0:T(4,128)(2,1)} %copy.19), kind=kOutput, calls=%fused_computation.4.clone.1 | convolution fusion | flops 9437184 | bytes 11824129 | tf_op jit(solution)/shard_map/while/body/eval_jaxpr/abn,nbr->nar/dot_general | solution.py:14
  187.6 9.3 %select_add_fusion.2 = f32[1536,3,256]{2,1,0:T(4,128)} fusion(f32[1536,3,256]{2,1,0:T(4,128)} %get-tuple-element.177, pred[]{:T(512)S(6)} %compare.5, bf16[3,3,1536]{1,0,2:T(4,128)(2,1)} %copy.17, bf16[1536,3,256]{2,1,0:T(4,128)(2,1)} %copy.19), kind=kOutput, calls=%fused_computation.4.clone.1 | convolution fusion | flops 9437184 | bytes 11824129 | tf_op jit(solution)/shard_map/while/body/eval_jaxpr/abn,nbr->nar/dot_general | solution.py:14
  216.5 9.3 %select_add_fusion.2 = f32[1536,3,256]{2,1,0:T(4,128)} fusion(f32[1536,3,256]{2,1,0:T(4,128)} %get-tuple-element.177, pred[]{:T(512)S(6)} %compare.5, bf16[3,3,1536]{1,0,2:T(4,128)(2,1)} %copy.17, bf16[1536,3,256]{2,1,0:T(4,128)(2,1)} %copy.19), kind=kOutput, calls=%fused_computation.4.clone.1 | convolution fusion | flops 9437184 | bytes 11824129 | tf_op jit(solution)/shard_map/while/body/eval_jaxpr/abn,nbr->nar/dot_general | solution.py:14
  245.4 9.3 %select_add_fusion.2 = f32[1536,3,256]{2,1,0:T(4,128)} fusion(f32[1536,3,256]{2,1,0:T(4,128)} %get-tuple-element.177, pred[]{:T(512)S(6)} %compare.5, bf16[3,3,1536]{1,0,2:T(4,128)(2,1)} %copy.17, bf16[1536,3,256]{2,1,0:T(4,128)(2,1)} %copy.19), kind=kOutput, calls=%fused_computation.4.clone.1 | convolution fusion | flops 9437184 | bytes 11824129 | tf_op jit(solution)/shard_map/while/body/eval_jaxpr/abn,nbr->nar/dot_general | solution.py:14
  265.5 5.7 copy.19
  274.3 9.3 %select_add_fusion.2 = f32[1536,3,256]{2,1,0:T(4,128)} fusion(f32[1536,3,256]{2,1,0:T(4,128)} %get-tuple-element.177, pred[]{:T(512)S(6)} %compare.5, bf16[3,3,1536]{1,0,2:T(4,128)(2,1)} %copy.17, bf16[1536,3,256]{2,1,0:T(4,128)(2,1)} %copy.19), kind=kOutput, calls=%fused_computation.4.clone.1 | convolution fusion | flops 9437184 | bytes 11824129 | tf_op jit(solution)/shard_map/while/body/eval_jaxpr/abn,nbr->nar/dot_general | solution.py:14
  294.4 5.7 copy.19
  303.2 9.3 %select_add_fusion.2 = f32[1536,3,256]{2,1,0:T(4,128)} fusion(f32[1536,3,256]{2,1,0:T(4,128)} %get-tuple-element.177, pred[]{:T(512)S(6)} %compare.5, bf16[3,3,1536]{1,0,2:T(4,128)(2,1)} %copy.17, bf16[1536,3,256]{2,1,0:T(4,128)(2,1)} %copy.19), kind=kOutput, calls=%fused_computation.4.clone.1 | convolution fusion | flops 9437184 | bytes 11824129 | tf_op jit(solution)/shard_map/while/body/eval_jaxpr/abn,nbr->nar/dot_general | solution.py:14
  323.3 5.7 copy.19
  332.1 9.3 %select_add_fusion.2 = f32[1536,3,256]{2,1,0:T(4,128)} fusion(f32[1536,3,256]{2,1,0:T(4,128)} %get-tuple-element.177, pred[]{:T(512)S(6)} %compare.5, bf16[3,3,1536]{1,0,2:T(4,128)(2,1)} %copy.17, bf16[1536,3,256]{2,1,0:T(4,128)(2,1)} %copy.19), kind=kOutput, calls=%fused_computation.4.clone.1 | convolution fusion | flops 9437184 | bytes 11824129 | tf_op jit(solution)/shard_map/while/body/eval_jaxpr/abn,nbr->nar/dot_general | solution.py:14
  361.0 9.3 %select_add_fusion.2 = f32[1536,3,256]{2,1,0:T(4,128)} fusion(f32[1536,3,256]{2,1,0:T(4,128)} %get-tuple-element.177, pred[]{:T(512)S(6)} %compare.5, bf16[3,3,1536]{1,0,2:T(4,128)(2,1)} %copy.17, bf16[1536,3,256]{2,1,0:T(4,128)(2,1)} %copy.19), kind=kOutput, calls=%fused_computation.4.clone.1 | convolution fusion | flops 9437184 | bytes 11824129 | tf_op jit(solution)/shard_map/while/body/eval_jaxpr/abn,nbr->nar/dot_general | solution.py:14
  389.9 9.3 %select_add_fusion.2 = f32[1536,3,256]{2,1,0:T(4,128)} fusion(f32[1536,3,256]{2,1,0:T(4,128)} %get-tuple-element.177, pred[]{:T(512)S(6)} %compare.5, bf16[3,3,1536]{1,0,2:T(4,128)(2,1)} %copy.17, bf16[1536,3,256]{2,1,0:T(4,128)(2,1)} %copy.19), kind=kOutput, calls=%fused_computation.4.clone.1 | convolution fusion | flops 9437184 | bytes 11824129 | tf_op jit(solution)/shard_map/while/body/eval_jaxpr/abn,nbr->nar/dot_general | solution.py:14
  418.8 9.3 %select_add_fusion.2 = f32[1536,3,256]{2,1,0:T(4,128)} fusion(f32[1536,3,256]{2,1,0:T(4,128)} %get-tuple-element.177, pred[]{:T(512)S(6)} %compare.5, bf16[3,3,1536]{1,0,2:T(4,128)(2,1)} %copy.17, bf16[1536,3,256]{2,1,0:T(4,128)(2,1)} %copy.19), kind=kOutput, calls=%fused_computation.4.clone.1 | convolution fusion | flops 9437184 | bytes 11824129 | tf_op jit(solution)/shard_map/while/body/eval_jaxpr/abn,nbr->nar/dot_general | solution.py:14
  447.7 9.3 %select_add_fusion.2 = f32[1536,3,256]{2,1,0:T(4,128)} fusion(f32[1536,3,256]{2,1,0:T(4,128)} %get-tuple-element.177, pred[]{:T(512)S(6)} %compare.5, bf16[3,3,1536]{1,0,2:T(4,128)(2,1)} %copy.17, bf16[1536,3,256]{2,1,0:T(4,128)(2,1)} %copy.19), kind=kOutput, calls=%fused_computation.4.clone.1 | convolution fusion | flops 9437184 | bytes 11824129 | tf_op jit(solution)/shard_map/while/body/eval_jaxpr/abn,nbr->nar/dot_general | solution.py:14
  476.6 9.3 %select_add_fusion.2 = f32[1536,3,256]{2,1,0:T(4,128)} fusion(f32[1536,3,256]{2,1,0:T(4,128)} %get-tuple-element.177, pred[]{:T(512)S(6)} %compare.5, bf16[3,3,1536]{1,0,2:T(4,128)(2,1)} %copy.17, bf16[1536,3,256]{2,1,0:T(4,128)(2,1)} %copy.19), kind=kOutput, calls=%fused_computation.4.clone.1 | convolution fusion | flops 9437184 | bytes 11824129 | tf_op jit(solution)/shard_map/while/body/eval_jaxpr/abn,nbr->nar/dot_general | solution.py:14
  505.5 9.3 %select_add_fusion.2 = f32[1536,3,256]{2,1,0:T(4,128)} fusion(f32[1536,3,256]{2,1,0:T(4,128)} %get-tuple-element.177, pred[]{:T(512)S(6)} %compare.5, bf16[3,3,1536]{1,0,2:T(4,128)(2,1)} %copy.17, bf16[1536,3,256]{2,1,0:T(4,128)(2,1)} %copy.19), kind=kOutput, calls=%fused_computation.4.clone.1 | convolution fusion | flops 9437184 | bytes 11824129 | tf_op jit(solution)/shard_map/while/body/eval_jaxpr/abn,nbr->nar/dot_general | solution.py:14
  526.8 87.9 %all-reduce.2.cloned.1.call-done = f32[256,256]{0,1:T(8,128)} async-done(((f32[256,256]{0,1:T(8,128)}), f32[256,256]{0,1:T(8,128)}) %all-reduce.2.cloned.1.call-update) | async-done | bytes 262160 | tf_op jit(solution)/shard_map/psum | solution.py:50
  (151 shorter events, 325.0 us)
Async XLA Ops:
  13.8 12.5 %copy-start = (bf16[1536,768]{1,0:T(8,128)(2,1)S(1)}, bf16[1536,768]{1,0:T(8,128)(2,1)}, u32[]{:S(2)}) copy-start(bf16[1536,768]{1,0:T(8,128)(2,1)} %param.8) | copy-start | bytes 7077892
  19.0 31.7 %all-to-all-start = ((bf16[8,80,768]{2,1,0:T(8,128)(2,1)}), bf16[8,80,768]{2,1,0:T(8,128)(2,1)S(1)}, u32[]{:S(2)}, u32[]{:S(2)}) async-start(bf16[8,80,768]{2,1,0:T(8,128)(2,1)} %scatter_fusion), calls=%async_computation | async-start | bytes 1966080 | tf_op jit(solution)/shard_map/all_to_all | solution.py:40
  26.2 4.7 copy-start.1
  26.2 588.4 %all-reduce.2.cloned.1.call-start = ((), (), s32[]{:S(2)}) async-start(), calls=%async_computation.1 | async-start | bytes 524288 | tf_op jit(solution)/shard_map/psum | solution.py:50
Sparse Core Ops, SparseCore 0:
  526.9 87.7 all-reduce.1
where the time goes:
time: 628 us; the launch traced here: 623 us
  local copies, waits for them, and re-layouts  321 us (51%)
  matrix products  151 us (24%)
  waiting for transfers between devices  108 us (17%)
  other arithmetic  22.9 us (4%)
  between operations  13.5 us (2%)
  starting transfers between devices  7.31 us (1%)
    gather x32, local copies, waits for them, and re-layouts, one_slot(): picked = extended[columns[slot_index]].reshape(node_count, 3, width)  159 us
    dot_general x16, matrix products, one_slot(): jnp.einsum('abn,nbr->nar', matrix, picked, preferred_element_type=jnp.flo...  147 us
    reshape x16, local copies, waits for them, and re-layouts, one_slot(): picked = extended[columns[slot_index]].reshape(node_count, 3, width)  91.5 us
    psum x1, waiting for transfers between devices, on_device(): summed = lax.psum(partial_term, ('dom', 'grp'))  87.9 us
    squeeze x32, local copies, waits for them, and re-layouts, one_slot(): matrix = blocks[:, slot_index].reshape(3, 3, node_count)  36.5 us
    all_to_all x1, waiting for transfers between devices, on_device(): lax.all_to_all(padded, 'dom', split_axis=0, concat_axis=0, tiled=True)  19.7 us
    select_n x16, other arithmetic, one_slot(): picked = extended[columns[slot_index]].reshape(node_count, 3, width)  13.2 us
    dynamic_slice x16, local copies, waits for them, and re-layouts, one_slot(): matrix = blocks[:, slot_index].reshape(3, 3, node_count)  12.8 us
  transfers between devices with their start and end apart: 2, of which 2 were waited for; matrix products, arithmetic and copies ran while one was open for 1% of the time, Pallas kernels for 0%

commit v1 on v0

v1 whole, which is shorter than its diff:
```python
import functools

import jax
import jax.numpy as jnp
from jax import lax
from jax.experimental import pallas as pl
from jax.experimental.pallas import tpu as pltpu
from jax.sharding import PartitionSpec as P

EDGE = 384
TILE = 256
LANES = 128
SUB = 16
F32 = jnp.float32
BF16 = jnp.bfloat16
MESH = pl.DeviceIdType.MESH


def offset_list(neighbours, group_size):
    reach = neighbours // 2
    half_way = group_size // 2
    offsets = [step + 1 for step in range(reach - 1)] + [half_way]
    return offsets + [-(step + 1) for step in range(reach - 1)] + [half_way + 1]


def kernel(
    n, basis_ref, blocks_ref, columns_ref, list_ref, counts_ref, out_ref,
    listpad, picks, outgoing, ghost, colsd, blocksd, wide, rel, kt_a, kt_b, vr, y, term4, sib, summed, landed,
    gsend, grecv, ssend, srecv, rsend, rrecv,
):
    nodes = basis_ref.shape[0]
    width = basis_ref.shape[1] // 3
    nnz = columns_ref.shape[0]
    neighbours, slots = list_ref.shape[1], list_ref.shape[2]
    half_share = sib.shape[1]
    own_tiles = nodes // TILE
    ghost_rows = ghost.shape[0]
    ghost_tiles = ghost_rows // TILE
    parts_me = lax.axis_index("parts")
    me = lax.axis_index("dom")
    grp = lax.axis_index("grp")
    other = 1 - grp
    offsets = offset_list(neighbours, n)

    barrier = pltpu.get_barrier_semaphore()
    pl.semaphore_signal(barrier, inc=1, device_id=(parts_me, me, other), device_id_type=MESH)

    def greet(step, carry):
        to = lax.rem(me + step, n)
        pl.semaphore_signal(barrier, inc=1, device_id=(parts_me, to, 0), device_id_type=MESH)
        pl.semaphore_signal(barrier, inc=1, device_id=(parts_me, to, 1), device_id_type=MESH)
        return carry

    lax.fori_loop(1, n, greet, 0)

    listpad[...] = jnp.full_like(listpad, -1.0)
    lane = lax.broadcasted_iota(jnp.int32, (1, slots), 1)
    for q in range(neighbours):
        row = jnp.where(lane < counts_ref[0, q], list_ref[0, q:q + 1, :], -1)
        listpad[q:q + 1, 0:slots] = row.astype(F32)
    turned = jnp.transpose(listpad[...])
    node_id = lax.broadcasted_iota(jnp.int32, (slots, nodes), 1).astype(F32)
    for q in range(neighbours):
        hit = jnp.broadcast_to(turned[0:slots, q:q + 1], (slots, nodes)) == node_id
        picks[q * slots:(q + 1) * slots, :] = jnp.where(hit, 1.0, 0.0).astype(BF16)
    for piece in range(3):
        cut = slice(piece * width, (piece + 1) * width)
        outgoing[:, cut] = jnp.dot(picks[...], basis_ref[:, cut], preferred_element_type=F32).astype(BF16)
    if ghost_rows > neighbours * slots:
        pad = ghost_rows - neighbours * slots
        ghost[neighbours * slots:, :] = jnp.zeros((pad, 3 * width), BF16)

    pl.semaphore_wait(barrier, 2 * n - 1)

    def ghost_copy(q):
        to = lax.rem(me + (offsets[q] + n), n)
        return pltpu.make_async_remote_copy(
            src_ref=outgoing.at[pl.ds(q * slots, slots)],
            dst_ref=ghost.at[pl.ds(q * slots, slots)],
            send_sem=gsend.at[q],
            recv_sem=grecv.at[q],
            device_id=(parts_me, to, grp),
            device_id_type=MESH,
        )

    for q in range(neighbours):
        ghost_copy(q).start()

    colsd[0:nnz, :] = columns_ref[...]
    colsd[nnz:2 * nnz, :] = columns_ref[...]

    def widen(tile, carry):
        lanes = pl.ds(pl.multiple_of(tile * LANES, LANES), LANES)
        for ab in range(9):
            value = blocks_ref[ab, :, lanes].astype(F32)
            blocksd[ab, 0:nnz, :] = value
            blocksd[ab, nnz:2 * nnz, :] = value
        mine = colsd[0:nnz, lanes]
        sums = [blocksd[ab, 0:nnz, :] for ab in range(9)]
        for shift in range(1, nnz):
            same = mine == colsd[shift:shift + nnz, lanes]
            for ab in range(9):
                sums[ab] = sums[ab] + jnp.where(same, blocksd[ab, shift:shift + nnz, :], 0.0)
        for ab in range(9):
            for slot in range(nnz):
                line = jnp.broadcast_to(sums[ab][slot:slot + 1, :], (SUB, LANES))
                wide[ab, slot, :, lanes] = line.astype(BF16)
        return carry

    lax.fori_loop(0, nodes // LANES, widen, 0)

    for chunk in range(own_tiles):
        for a in range(3):
            vr[chunk, a * TILE:(a + 1) * TILE, :] = basis_ref[
                chunk * TILE:(chunk + 1) * TILE, a * width:(a + 1) * width
            ]

    def clear(tile, carry):
        y[tile] = jnp.zeros((3 * TILE, width), F32)
        return carry

    lax.fori_loop(0, own_tiles + ghost_tiles, clear, 0)
    kt_b[...] = jnp.zeros_like(kt_b)

    base = (
        lax.broadcasted_iota(jnp.int32, (4, SUB, LANES), 0) * SUB
        + lax.broadcasted_iota(jnp.int32, (4, SUB, LANES), 1)
    )

    def build(tile, chunk, kt):
        for part in range(TILE // LANES):
            lanes = pl.ds(pl.multiple_of(chunk * TILE + part * LANES, LANES), LANES)
            near = (columns_ref[:, lanes] - tile * TILE).astype(F32)
            for slot in range(nnz):
                rel[part, slot] = jnp.broadcast_to(near[slot:slot + 1, :], (SUB, LANES)).astype(BF16)
            for quarter in range(4):
                rows = (base + quarter * 4 * SUB).astype(F32).astype(BF16)
                accs = [jnp.zeros((4, SUB, LANES), BF16) for _ in range(9)]
                for slot in range(nnz):
                    hit = jnp.broadcast_to(rel[part, slot][None], (4, SUB, LANES)) == rows
                    for ab in range(9):
                        value = jnp.broadcast_to(wide[ab, slot, :, lanes][None], (4, SUB, LANES))
                        accs[ab] = jnp.where(hit, value, accs[ab])
                for ab in range(9):
                    a, b = ab // 3, ab % 3
                    top = b * TILE + quarter * 4 * SUB
                    left = a * TILE + part * LANES
                    kt[top:top + 4 * SUB, left:left + LANES] = accs[ab].reshape(4 * SUB, LANES)

    def multiply(tile, chunk, kt):
        y[tile] += jnp.dot(kt[...], vr[chunk], preferred_element_type=F32)

    own_pairs = own_tiles // 2
    own_steps = own_tiles * own_pairs
    edge_chunk = (nodes - EDGE) // TILE // 2 * 2
    edge_pairs = (own_tiles - edge_chunk) // 2
    steps = own_steps + ghost_tiles * edge_pairs

    def place(step):
        late = step // own_steps
        tile = (1 - late) * (step // own_pairs) + late * (own_tiles + (step - own_steps) // edge_pairs)
        chunk = (1 - late) * (2 * (step % own_pairs)) + late * (edge_chunk + 2 * (step % edge_pairs))
        return tile, chunk

    def advance(step, carry):
        tile, chunk = place(step)
        tile_before, chunk_before = place((step + steps - 1) % steps)
        build(tile, chunk, kt_a)
        multiply(tile_before, chunk_before + 1, kt_b)
        build(tile, chunk + 1, kt_b)
        multiply(tile, chunk, kt_a)
        return carry

    lax.fori_loop(0, steps, advance, 0)
    tile_last, chunk_last = place(steps - 1)
    multiply(tile_last, chunk_last + 1, kt_b)

    turn = (((0,), (0,)), ((), ()))

    def fold(tile, total):
        return total + lax.dot_general(y[tile].astype(BF16), vr[tile], turn, preferred_element_type=F32)

    total = lax.fori_loop(0, own_tiles, fold, jnp.zeros((width, width), F32))
    for q in range(neighbours):
        ghost_copy(q).wait_recv()
    for tile in range(ghost_tiles):
        for b in range(3):
            total = total + lax.dot_general(
                y[own_tiles + tile, b * TILE:(b + 1) * TILE, :].astype(BF16),
                ghost[tile * TILE:(tile + 1) * TILE, b * width:(b + 1) * width],
                turn,
                preferred_element_type=F32,
            )
    for to in range(n):
        for half in range(2):
            top = (2 * to + half) * half_share
            term4[half, to] = total[top:top + half_share, :]

    pair = pltpu.make_async_remote_copy(
        src_ref=term4.at[other],
        dst_ref=sib,
        send_sem=ssend,
        recv_sem=srecv,
        device_id=(parts_me, me, other),
        device_id_type=MESH,
    )
    pair.start()
    pair.wait_recv()
    summed[...] = term4[grp] + sib[...]

    def share_copy(to, to_grp):
        return pltpu.make_async_remote_copy(
            src_ref=summed.at[to],
            dst_ref=landed.at[grp, me],
            send_sem=rsend.at[to_grp, to],
            recv_sem=rrecv.at[grp, me],
            device_id=(parts_me, to, to_grp),
            device_id_type=MESH,
        )

    def arrival(half, source):
        return pltpu.make_async_remote_copy(
            src_ref=summed.at[source],
            dst_ref=landed.at[half, source],
            send_sem=rsend.at[half, source],
            recv_sem=rrecv.at[half, source],
            device_id=(parts_me, source, half),
            device_id_type=MESH,
        )

    def send(step, carry):
        to = lax.rem(me + step, n)
        share_copy(to, 0).start()
        share_copy(to, 1).start()
        return carry

    lax.fori_loop(1, n, send, 0)
    share_copy(me, other).start()
    landed[grp, me] = summed[me]

    def receive(step, carry):
        source = lax.rem(me + step, n)
        arrival(0, source).wait_recv()
        arrival(1, source).wait_recv()
        return carry

    lax.fori_loop(1, n, receive, 0)
    arrival(other, me).wait_recv()
    for half in range(2):
        out_ref[half * half_share:(half + 1) * half_share, :] = jnp.sum(landed[half], axis=0)

    for q in range(neighbours):
        ghost_copy(q).wait_send()
    pair.wait_send()

    def sent(step, carry):
        to = lax.rem(me + step, n)
        share_copy(to, 0).wait_send()
        share_copy(to, 1).wait_send()
        return carry

    lax.fori_loop(1, n, sent, 0)
    share_copy(me, other).wait_send()


def on_device(basis, blocks, columns, send_list, send_counts):
    nodes, width = basis.shape[0], basis.shape[1] // 3
    nnz = columns.shape[0]
    neighbours, slots = send_list.shape[1], send_list.shape[2]
    n = lax.axis_size("dom")
    share = width // n
    half = share // 2
    own_tiles = nodes // TILE
    ghost_tiles = -(-neighbours * slots // TILE)
    vmem = pl.BlockSpec(memory_space=pltpu.VMEM)
    return pl.pallas_call(
        functools.partial(kernel, n),
        out_shape=jax.ShapeDtypeStruct((share, width), F32),
        in_specs=[vmem, vmem, vmem, vmem, pl.BlockSpec(memory_space=pltpu.SMEM)],
        out_specs=vmem,
        scratch_shapes=[
            pltpu.VMEM((LANES, LANES), F32),
            pltpu.VMEM((neighbours * slots, nodes), BF16),
            pltpu.VMEM((neighbours * slots, 3 * width), BF16),
            pltpu.VMEM((ghost_tiles * TILE, 3 * width), BF16),
            pltpu.VMEM((2 * nnz, nodes), jnp.int32),
            pltpu.VMEM((9, 2 * nnz, LANES), F32),
            pltpu.VMEM((9, nnz, SUB, nodes), BF16),
            pltpu.VMEM((2, nnz, SUB, LANES), BF16),
            pltpu.VMEM((3 * TILE, 3 * TILE), BF16),
            pltpu.VMEM((3 * TILE, 3 * TILE), BF16),
            pltpu.VMEM((own_tiles, 3 * TILE, width), BF16),
            pltpu.VMEM((own_tiles + ghost_tiles, 3 * TILE, width), F32),
            pltpu.VMEM((2, n, half, width), F32),
            pltpu.VMEM((n, half, width), F32),
            pltpu.VMEM((n, half, width), F32),
            pltpu.VMEM((2, n, half, width), F32),
            pltpu.SemaphoreType.DMA((neighbours,)),
            pltpu.SemaphoreType.DMA((neighbours,)),
            pltpu.SemaphoreType.DMA,
            pltpu.SemaphoreType.DMA,
            pltpu.SemaphoreType.DMA((2, n)),
            pltpu.SemaphoreType.DMA((2, n)),
        ],
        compiler_params=pltpu.CompilerParams(
            collective_id=0, has_side_effects=True, vmem_limit_bytes=56 * 1024 * 1024
        ),
    )(basis, blocks, columns, send_list, send_counts)


def solution(mesh):
    in_specs = (
        P(("parts", "dom", "grp"), None),
        P(None, None, ("parts", "dom", "grp")),
        P(None, ("parts", "dom", "grp")),
        P(("parts", "dom", "grp"), None, None),
        P(("parts", "dom", "grp"), None),
    )
    out_specs = P(("parts", "dom"), None)
    return jax.shard_map(
        on_device, mesh=mesh, in_specs=in_specs, out_specs=out_specs, check_vma=False
    )
```

time: 628 us -> 190 us (0.30)
  local copies, waits for them, and re-layouts: 321 us -> 2.65 us
  Pallas kernels: 0 us -> 187 us
  matrix products: 151 us -> 0 us
  waiting for transfers between devices: 108 us -> 0 us
  other arithmetic: 22.9 us -> 0 us
  between operations: 13.5 us -> 0.01 us
  starting transfers between devices: 7.31 us -> 0 us
    pallas_call x0 -> x1, Pallas kernels: none -> 187 us  [on_device(): pl.pallas_call(functools.partial(kernel, n), out_shape=jax.ShapeDtypeStru...]
    gather x34 -> x0, local copies, waits for them, and re-layouts: 166 us -> none  [the longest x32 159 us: one_slot(): picked = extended[columns[slot_index]].reshape(node_count, 3, width)]
    dot_general x17 -> x0, matrix products: 151 us -> none  [the longest x16 147 us: one_slot(): jnp.einsum('abn,nbr->nar', matrix, picked, preferred_element_type=jnp.flo...]
    reshape x18 -> x0, local copies, waits for them, and re-layouts: 98 us -> none  [the longest x16 91.5 us: one_slot(): picked = extended[columns[slot_index]].reshape(node_count, 3, width)]
    psum x1 -> x0, waiting for transfers between devices: 87.9 us -> none  [on_device(): summed = lax.psum(partial_term, ('dom', 'grp'))]
    squeeze x32 -> x0, local copies, waits for them, and re-layouts: 36.5 us -> none  [one_slot(): matrix = blocks[:, slot_index].reshape(3, 3, node_count)]
    all_to_all x1 -> x0, waiting for transfers between devices: 19.7 us -> none  [on_device(): lax.all_to_all(padded, 'dom', split_axis=0, concat_axis=0, tiled=True)]
    select_n x19 -> x0, other arithmetic: 14.6 us -> none  [the longest x16 13.2 us: one_slot(): picked = extended[columns[slot_index]].reshape(node_count, 3, width)]
  transfers between devices with their start and end apart: 2 -> 0, of which waited for: 2 -> 0; matrix products, arithmetic and copies ran while one was open for 1% -> 0% of each run, Pallas kernels for 0% -> 0%
where the time goes in v1:
time: 190 us; the launch traced here: 189 us
  Pallas kernels  187 us (98%)
  local copies, waits for them, and re-layouts  2.65 us (1%)
    pallas_call x1, Pallas kernels, on_device(): pl.pallas_call(functools.partial(kernel, n), out_shape=jax.ShapeDtypeStru...  187 us

profile of v1, /device:TPU:0, one launch (start us, length us, event | category | flops | bytes accessed | tf_op | source)
XLA Modules:
  0.0 189.3 jit_solution(8267421655895013174)
XLA Ops:
  0.0 1.3 copy.6.list_ref
  1.3 186.6 %shard_map.55 = f32[32,256]{1,0:T(8,128)} custom-call(bf16[1536,768]{1,0:T(8,128)(2,1)} %basis_ref.1, bf16[9,16,1536]{2,1,0:T(8,128)(2,1)} %blocks_ref.1, s32[16,1536]{1,0:T(8,128)} %columns_ref.1, s32[1,6,80]{2,1,0:T(8,128)} %copy.6.list_ref, s32[1,6]{1,0:T(1,128)} %counts_ref.1), custom_call_target="tpu_custom_call" | custom-call | tf_op jit(solution)/shard_map/pallas_call | solution.py:276
  187.9 1.4 copy.8

commit v2 on v1

--- a/solution.py
+++ b/solution.py
@@ -127,25 +127,39 @@
         + lax.broadcasted_iota(jnp.int32, (4, SUB, LANES), 1)
     )
 
-    def build(tile, chunk, kt):
+    def near_rows(tile, chunk):
         for part in range(TILE // LANES):
             lanes = pl.ds(pl.multiple_of(chunk * TILE + part * LANES, LANES), LANES)
             near = (columns_ref[:, lanes] - tile * TILE).astype(F32)
             for slot in range(nnz):
                 rel[part, slot] = jnp.broadcast_to(near[slot:slot + 1, :], (SUB, LANES)).astype(BF16)
-            for quarter in range(4):
-                rows = (base + quarter * 4 * SUB).astype(F32).astype(BF16)
-                accs = [jnp.zeros((4, SUB, LANES), BF16) for _ in range(9)]
+
+    def build_rows(chunk, quarter, part, kt):
+        rows = (base + quarter * 4 * SUB).astype(F32).astype(BF16)
+        if True:
+            lanes = pl.ds(pl.multiple_of(chunk * TILE + part * LANES, LANES), LANES)
+            for b in range(3):
+                accs = [jnp.zeros((4, SUB, LANES), BF16) for _ in range(3)]
                 for slot in range(nnz):
                     hit = jnp.broadcast_to(rel[part, slot][None], (4, SUB, LANES)) == rows
-                    for ab in range(9):
-                        value = jnp.broadcast_to(wide[ab, slot, :, lanes][None], (4, SUB, LANES))
-                        accs[ab] = jnp.where(hit, value, accs[ab])
-                for ab in range(9):
-                    a, b = ab // 3, ab % 3
-                    top = b * TILE + quarter * 4 * SUB
-                    left = a * TILE + part * LANES
-                    kt[top:top + 4 * SUB, left:left + LANES] = accs[ab].reshape(4 * SUB, LANES)
+                    for a in range(3):
+                        value = jnp.broadcast_to(wide[3 * a + b, slot, :, lanes][None], (4, SUB, LANES))
+                        accs[a] = jnp.where(hit, value, accs[a])
+                for a in range(3):
+                    top = pl.multiple_of(b * TILE + quarter * 4 * SUB, 4 * SUB)
+                    left = pl.multiple_of(a * TILE + part * LANES, LANES)
+                    kt[pl.ds(top, 4 * SUB), pl.ds(left, LANES)] = accs[a].reshape(4 * SUB, LANES)
+
+    def build_and_multiply(tile, chunk, kt, tile_before, chunk_before, kt_before):
+        near_rows(tile, chunk)
+
+        def one(step, carry):
+            build_rows(chunk, step // 2, step % 2, kt)
+            cut = pl.ds(pl.multiple_of(step * (3 * TILE // 8), 3 * TILE // 8), 3 * TILE // 8)
+            y[tile_before, cut, :] += jnp.dot(kt_before[cut, :], vr[chunk_before], preferred_element_type=F32)
+            return carry
+
+        lax.fori_loop(0, 8, one, 0)
 
     def multiply(tile, chunk, kt):
         y[tile] += jnp.dot(kt[...], vr[chunk], preferred_element_type=F32)
@@ -165,10 +179,8 @@
     def advance(step, carry):
         tile, chunk = place(step)
         tile_before, chunk_before = place((step + steps - 1) % steps)
-        build(tile, chunk, kt_a)
-        multiply(tile_before, chunk_before + 1, kt_b)
-        build(tile, chunk + 1, kt_b)
-        multiply(tile, chunk, kt_a)
+        build_and_multiply(tile, chunk, kt_a, tile_before, chunk_before + 1, kt_b)
+        build_and_multiply(tile, chunk + 1, kt_b, tile, chunk, kt_a)
         return carry
 
     lax.fori_loop(0, steps, advance, 0)

time: 190 us -> 106 us (0.56)
  Pallas kernels: 187 us -> 103 us
    pallas_call x1, Pallas kernels: 187 us -> 103 us  [on_device(): pl.pallas_call(functools.partial(kernel, n), out_shape=jax.ShapeDtypeStru...]
where the time goes in v2:
time: 106 us
  Pallas kernels  103 us (97%)
  local copies, waits for them, and re-layouts  2.65 us (2%)
    pallas_call x1, Pallas kernels, on_device(): pl.pallas_call(functools.partial(kernel, n), out_shape=jax.ShapeDtypeStru...  103 us
    unnamed x2, local copies, waits for them, and re-layouts  2.65 us

profile of v2, /device:TPU:0, one launch (start us, length us, event | category | flops | bytes accessed | tf_op | source)
XLA Modules:
  0.0 105.5 jit_solution(1332956528946468711)
XLA Ops:
  0.0 1.3 %copy.6.list_ref = s32[1,6,80]{2,1,0:T(8,128)} copy(s32[1,6,80]{2,0,1:T(1,128)} %param.8) | data formatting | bytes 3840 | tf_op args[3]
  1.3 102.9 %shard_map.55 = f32[32,256]{1,0:T(8,128)} custom-call(bf16[1536,768]{1,0:T(8,128)(2,1)} %basis_ref.1, bf16[9,16,1536]{2,1,0:T(8,128)(2,1)} %blocks_ref.1, s32[16,1536]{1,0:T(8,128)} %columns_ref.1, s32[1,6,80]{2,1,0:T(8,128)} %copy.6.list_ref, s32[1,6]{1,0:T(1,128)} %counts_ref.1), custom_call_target="tpu_custom_call" | custom-call | tf_op jit(solution)/shard_map/pallas_call | solution.py:288
  104.2 1.4 %copy.8 = f32[32,256]{1,0:T(8,128)} copy(f32[32,256]{1,0:T(8,128)} %shard_map.55) | data formatting | bytes 65536
